TPU v7x, 32 devices: a whole 2x2x4 slice. The times are simulated.
32 devices in a mesh: groups: 2 (over y), sub: 4 (over z), blk: 4 (over x, core).
Axes of the slice: x: 2, y: 2, z: 4, core: 2. Of those that a mesh axis runs over, the one named last changes fastest.
Arguments:
- conductance: float32 [128, 8192], P(('groups', 'sub'), 'blk'), parts along dimension 0, may hold values from 0.1 to 10
- source_mask: int32 [128, 8192], P(('groups', 'sub'), 'blk'), parts along dimension 0, may hold values 0 or 1
- ground_mask: int32 [128, 8192], P(('groups', 'sub'), 'blk'), parts along dimension 0, may hold values 0 or 1
- nodata_mask: int32 [128, 8192], P(('groups', 'sub'), 'blk'), parts along dimension 0, may hold values 0 or 1
Outputs:
- potential: float32 [128, 8192], P(('groups', 'sub'), 'blk'), parts along dimension 0
There are 2 independent parts, one for each index of `groups`. A program takes and returns all parts, laid end to end along the dimension named above; each array names one. Nothing has to cross between parts.
All inputs are finite; a program needn't handle non-finite values. No bound on the sum of `source_mask` or of `ground_mask` or of `nodata_mask` on one device may be relied on, other than what follows from the above.
Results may differ from a plain program's by a relative error of at most 0.0003.
Values sent between devices are 32-bit elements; how exact they have to be, the bound alone decides.
A program may use at most 64 MiB of HBM per device.

v0:
```python
import functools
import jax
import jax.numpy as jnp
from jax import lax
from jax.experimental import pallas as pl
from jax.experimental.pallas import tpu as pltpu
from jax.sharding import PartitionSpec as P

LEVELS = 5
SMOOTH = (2, 0.5, 2.0)
COARSE_LOW, COARSE_HIGH = 0.02, 2.0
DIRS = ((-1, 0), (1, 0), (0, -1), (0, 1), (-1, -1), (-1, 1), (1, -1), (1, 1))
MESH = pl.DeviceIdType.MESH


def round_up(n, k):
    return -(-n // k) * k


def chebyshev_terms(sweep_count, low_end, high_end):
    mid = 0.5 * (high_end + low_end)
    half = 0.5 * (high_end - low_end)
    sigma = mid / half
    rho = 1.0 / sigma
    terms = [(0.0, 1.0 / mid)]
    for _ in range(1, sweep_count):
        rho_next = 1.0 / (2.0 * sigma - rho)
        terms.append((rho_next * rho, 2.0 * rho_next / half))
        rho = rho_next
    return terms


def rolled(x, shift, axis):
    return pltpu.roll(x, shift % x.shape[axis], axis)


def level_operator(c, g, whole_rows):
    rows, cols = c.shape
    h = 0.5 * c
    valid = c > 0.0
    c_r = rolled(c, -1, 1)
    c_d = rolled(c, -1, 0)
    e_r = jnp.where(valid & (c_r > 0.0), h + 0.5 * c_r, 0.0)
    ok_d = valid & (c_d > 0.0)
    if whole_rows:
        ok_d = ok_d & (lax.broadcasted_iota(jnp.int32, c.shape, 0) < rows - 1)
    e_d = jnp.where(ok_d, h + 0.5 * c_d, 0.0)
    e_l = rolled(e_r, 1, 1)
    e_u = rolled(e_d, 1, 0)
    m = jnp.where(valid, 1.0, 0.0)
    diag = e_d + e_u + e_r + e_l + g + (1.0 - m)
    inv = 1.0 / jnp.maximum(diag, 0.25 * c)
    return e_r, e_l, e_d, e_u, diag, inv, m


def residual(op, f, x):
    e_r, e_l, e_d, e_u, diag, inv, m = op
    out = f - diag * x
    out = out + e_r * rolled(x, -1, 1) + e_l * rolled(x, 1, 1)
    return out + e_d * rolled(x, -1, 0) + e_u * rolled(x, 1, 0)


def smooth(op, f, x, terms):
    d = None
    for keep, fresh in terms:
        r = f if x is None else residual(op, f, x)
        step = fresh * (r * op[5])
        d = step if d is None else keep * d + step
        x = d if x is None else x + d
    return x


def lane_take(x, which):
    lane = lax.broadcasted_iota(jnp.int32, x.shape, 1)
    if which == 0:
        index = jnp.bitwise_and(2 * lane, 127)
    else:
        index = jnp.right_shift(lane, 1) + 64 * (which - 1)
    return jnp.take_along_axis(x, index, axis=1, mode="promise_in_bounds")


def coarsen(x, tmp):
    rows, cols = x.shape
    k = round_up(cols, 256) // 256
    half = rows // 2
    sums = []
    for odd in range(2):
        base = odd * rows * k
        for j in range(k):
            lanes = 256 * j + 128 * odd
            if lanes < cols:
                tile = x[:, lanes : lanes + 128]
            else:
                tile = jnp.zeros((rows, 128), jnp.float32)
            tmp[base + rows * j : base + rows * (j + 1), :] = tile
        t = tmp[pl.ds(base, half * k, stride=2), :] + tmp[pl.ds(base + 1, half * k, stride=2), :]
        sums.append(lane_take(t + rolled(t, -1, 1), 0))
    lane = lax.broadcasted_iota(jnp.int32, sums[0].shape, 1)
    s = jnp.where(lane < 64, *sums)
    return [s[half * j : half * (j + 1)] for j in range(k)]


def prolong(x, first, rows, tmp, cols):
    n = cols // 128
    for j in range(x.shape[1] // 128):
        tile = x[:, 128 * j : 128 * j + 128]
        for side in range(2):
            if 2 * j + side < n:
                base = 2 * rows * (2 * j + side)
                v = lane_take(tile, 1 + side)[first : first + rows]
                tmp[pl.ds(base, rows, stride=2), :] = v
                tmp[pl.ds(base + 1, rows, stride=2), :] = v
    return jnp.concatenate([tmp[2 * rows * j : 2 * rows * (j + 1), :] for j in range(n)], axis=1)


def kernel(
    plan,
    cond_h, src_h, gnd_h, nod_h, out, cond, nod, gnd, src, in_sem,
    c0, g0, f0, x0, c1, g1, f1, x1, c2, g2, f2, y2, f3, f4, tmp, tmp_up,
    a_row_s, a_row_r, a_col_s, a_col_r, a_cor_s, a_cor_r, a_sem,
    b_row_s, b_row_r, b_cor_s, b_cor_r, b_sem,
    x0_s, x0_r, f1_s, f1_r, x1_s, x1_r, row_sem,
    cg2_g, f2_g, gather_sem,
):
    n_sub, n_blk, halo, widths, coarse_count = plan
    s, b = lax.axis_index("sub"), lax.axis_index("blk")
    w0, w1, w2, w3, w4 = widths
    own = out.shape[1]

    def exists(dr, dc):
        ok = None
        for need, cond_ in (
            (dr < 0, s > 0), (dr > 0, s < n_sub - 1), (dc < 0, b > 0), (dc > 0, b < n_blk - 1),
        ):
            if need:
                ok = cond_ if ok is None else ok & cond_
        return ok

    loads = [
        pltpu.make_async_copy(a, v, in_sem.at[i])
        for i, (a, v) in enumerate(((cond_h, cond), (nod_h, nod), (gnd_h, gnd), (src_h, src)))
    ]
    for load in loads:
        load.start()

    barrier = pltpu.get_barrier_semaphore()
    for dr in range(n_sub):
        @pl.when(s != dr)
        def _():
            pl.semaphore_signal(barrier, 1, device_id={"sub": dr}, device_id_type=MESH)
    for dr, dc in DIRS[2:]:
        @pl.when(exists(dr, dc))
        def _():
            pl.semaphore_signal(
                barrier, 1, device_id={"sub": s + dr, "blk": b + dc}, device_id_type=MESH
            )

    for ref in (c0, g0, f0, c1, g1, f1, y2, f3, f4):
        ref[...] = jnp.zeros_like(ref)

    for load in loads:
        load.wait()
    valid = 1.0 - nod[...].astype(jnp.float32)
    c = cond[...] * valid
    g = gnd[...].astype(jnp.float32) * c
    f = valid * (src[...].astype(jnp.float32) - 0.125)
    c0[4:20, halo : halo + own] = c
    g0[4:20, halo : halo + own] = g
    f0[4:20, halo : halo + own] = f
    for i, (rc, rg) in enumerate(((slice(0, 3), slice(0, 2)), (slice(13, 16), slice(14, 16)))):
        a_row_s[i, 0:3] = c[rc]
        a_row_s[i, 3:5] = g[rg]
        a_row_s[i, 5:7] = f[rg]
        a_row_s[i, 7:8] = jnp.zeros((1, own), jnp.float32)
        for j, lanes in enumerate((slice(0, halo), slice(own - halo, own))):
            a_cor_s[2 * i + j, 0:3] = c[rc, lanes]
            a_cor_s[2 * i + j, 3:5] = g[rg, lanes]
            a_cor_s[2 * i + j, 5:7] = f[rg, lanes]
            a_cor_s[2 * i + j, 7:8] = jnp.zeros((1, halo), jnp.float32)
    for j, lanes in enumerate((slice(0, halo), slice(own - halo, own))):
        a_col_s[j, 0:16] = c[:, lanes]
        a_col_s[j, 16:32] = g[:, lanes]
        a_col_s[j, 32:48] = f[:, lanes]

    has = lambda flag: jnp.where(flag, 1, 0)
    partners = n_sub - 1
    for dr, dc in DIRS[2:]:
        partners = partners + has(exists(dr, dc))
    pl.semaphore_wait(barrier, partners)

    def remote(src_ref, dst_ref, send, recv, dr, dc=0):
        return pltpu.make_async_remote_copy(
            src_ref=src_ref, dst_ref=dst_ref, send_sem=send, recv_sem=recv,
            device_id={"sub": s + dr, "blk": b + dc}, device_id_type=MESH,
        )

    def a_copy(d):
        dr, dc = DIRS[d]
        if d < 2:
            pair_ = a_row_s.at[d], a_row_r.at[d]
        elif d < 4:
            pair_ = a_col_s.at[d - 2], a_col_r.at[d - 2]
        else:
            pair_ = a_cor_s.at[d - 4], a_cor_r.at[d - 4]
        return remote(*pair_, a_sem.at[0, d], a_sem.at[1, d], dr, dc)

    def b_copy(d):
        dr, dc = DIRS[d]
        pair_ = (b_row_s.at[d], b_row_r.at[d]) if d < 2 else (b_cor_s.at[d - 4], b_cor_r.at[d - 4])
        return remote(*pair_, b_sem.at[0, d], b_sem.at[1, d], dr, dc)

    row_bufs = ((x0_s, x0_r), (f1_s, f1_r), (x1_s, x1_r))

    def row_copy(e, d):
        send, recv = row_bufs[e]
        return remote(send.at[d], recv.at[d], row_sem.at[0, e, d], row_sem.at[1, e, d], DIRS[d][0])

    def row_start(e):
        for d in range(2):
            @pl.when(exists(*DIRS[d]))
            def _():
                row_copy(e, d).start()

    def row_wait(e, put):
        for d in range(2):
            @pl.when(exists(-DIRS[d][0], 0))
            def _():
                row_copy(e, d).wait_recv()
                put(d)

    def gather_copy(e, other, sender):
        buf = (cg2_g, f2_g)[e]
        return pltpu.make_async_remote_copy(
            src_ref=buf.at[sender], dst_ref=buf.at[sender],
            send_sem=gather_sem.at[0, e, other], recv_sem=gather_sem.at[1, e, sender],
            device_id={"sub": other}, device_id_type=MESH,
        )

    def gather_start(e):
        for other in range(n_sub):
            @pl.when(s != other)
            def _():
                gather_copy(e, other, s).start()

    def gather_wait(e):
        for other in range(n_sub):
            @pl.when(s != other)
            def _():
                gather_copy(e, other, other).wait_recv()

    for d in range(8):
        @pl.when(exists(*DIRS[d]))
        def _():
            a_copy(d).start()

    h1, own1 = halo // 2, own // 2
    both = jnp.concatenate([0.25 * c, g], axis=0)
    both = jnp.concatenate(coarsen(both, tmp), axis=1)
    c1[4:12, h1 : h1 + own1] = both[0:8]
    g1[4:12, h1 : h1 + own1] = both[8:16]
    for i, (rc, rg) in enumerate(((slice(0, 3), slice(8, 10)), (slice(5, 8), slice(14, 16)))):
        b_row_s[i, 0:3] = both[rc]
        b_row_s[i, 3:5] = both[rg]
        b_row_s[i, 5:8] = jnp.zeros((3, own1), jnp.float32)
        for j, lanes in enumerate((slice(0, h1), slice(own1 - h1, own1))):
            b_cor_s[2 * i + j, 0:3] = both[rc, lanes]
            b_cor_s[2 * i + j, 3:5] = both[rg, lanes]
            b_cor_s[2 * i + j, 5:8] = jnp.zeros((3, h1), jnp.float32)
    for d in (0, 1, 4, 5, 6, 7):
        @pl.when(exists(*DIRS[d]))
        def _():
            b_copy(d).start()

    for d, (dr, dc) in enumerate(DIRS):
        @pl.when(exists(-dr, -dc))
        def _():
            a_copy(d).wait_recv()
            lanes = {0: slice(halo, halo + own), 1: slice(0, halo), -1: slice(halo + own, w0)}[dc]
            if dr == 0:
                for k, ref in enumerate((c0, g0, f0)):
                    ref[4:20, lanes] = a_col_r[d - 2, 16 * k : 16 * k + 16]
            else:
                got = (a_row_r, d) if d < 2 else (a_cor_r, d - 4)
                got = got[0].at[got[1]]
                c0[slice(1, 4) if dr > 0 else slice(20, 23), lanes] = got[0:3]
                near = slice(2, 4) if dr > 0 else slice(20, 22)
                g0[near, lanes] = got[3:5]
                f0[near, lanes] = got[5:7]

    terms = chebyshev_terms(*SMOOTH)
    op0 = level_operator(c0[...], g0[...], False)
    f = f0[...]
    x = smooth(op0, f, None, terms)
    r = residual(op0, f, x)
    rhs = jnp.concatenate(coarsen(r[4:20], tmp), axis=1)
    f1[4:12, :] = rhs
    f1_s[0] = rhs[0:2]
    f1_s[1] = rhs[6:8]
    row_start(1)
    x0[...] = x
    x0_s[0] = x[4:6]
    x0_s[1] = x[18:20]
    row_start(0)

    sides = (slice(0, halo), slice(halo + own, w0))
    both = jnp.concatenate(
        [jnp.concatenate([0.25 * c0[4:20, v], g0[4:20, v]], axis=0) for v in sides], axis=1
    )
    both = jnp.concatenate(coarsen(both, tmp), axis=1)
    for k, lanes in enumerate((slice(0, h1), slice(h1 + own1, 2 * h1 + own1))):
        c1[4:12, lanes] = both[0:8, h1 * k : h1 * k + h1]
        g1[4:12, lanes] = both[8:16, h1 * k : h1 * k + h1]
    both = jnp.concatenate([0.25 * c1[4:12, :], g1[4:12, :]], axis=0)
    cg2_g[s] = jnp.concatenate(coarsen(both, tmp), axis=1)
    gather_start(0)
    for d in (0, 1, 4, 5, 6, 7):
        dr, dc = DIRS[d]
        @pl.when(exists(-dr, -dc))
        def _():
            b_copy(d).wait_recv()
            lanes = {0: slice(h1, h1 + own1), 1: slice(0, h1), -1: slice(h1 + own1, w1)}[dc]
            got = b_row_r.at[d] if d < 2 else b_cor_r.at[d - 4]
            c1[slice(1, 4) if dr > 0 else slice(12, 15), lanes] = got[0:3]
            g1[slice(2, 4) if dr > 0 else slice(12, 14), lanes] = got[3:5]
    op1 = level_operator(c1[...], g1[...], False)

    def put_f1(d):
        f1[slice(12, 14) if d == 0 else slice(2, 4), :] = f1_r[d]

    row_wait(1, put_f1)
    fl1 = f1[...]
    x = smooth(op1, fl1, None, terms)
    r = residual(op1, fl1, x)
    f2_g[s] = jnp.concatenate(coarsen(r[4:12], tmp), axis=1)
    gather_start(1)
    x1[...] = x
    x1_s[0] = x[4:7]
    x1_s[1] = x[9:12]
    row_start(2)

    gather_wait(0)
    for k in range(n_sub):
        c2[4 * k : 4 * k + 4, :] = cg2_g[k, 0:4]
        g2[4 * k : 4 * k + 4, :] = cg2_g[k, 4:8]

    cg = (c2[...], g2[...])
    ops = [level_operator(*cg, True)]
    rows = 4 * n_sub
    for level, width in ((3, w3), (4, w4)):
        rows //= 2
        full = max(rows, 8)
        parts = []
        for k, v in enumerate(cg):
            tiles = coarsen(0.25 * v if k == 0 else v, tmp)
            v = jnp.concatenate(tiles, axis=1)[:rows]
            if full > rows:
                v = jnp.concatenate([v, jnp.zeros((full - rows, width), jnp.float32)], axis=0)
            parts.append(v)
        cg = tuple(parts)
        ops.append(level_operator(*cg, True))

    gather_wait(1)
    for k in range(n_sub):
        f2[4 * k : 4 * k + 4, :] = f2_g[k]
    rhs = f2[...]
    kept = []
    rows = 4 * n_sub
    for level in (2, 3):
        op = ops[level - 2]
        x = smooth(op, rhs, None, terms)
        r = residual(op, rhs, x)
        kept.append((rhs, x))
        rows //= 2
        ref = (f3, f4)[level - 2]
        for j, tile in enumerate(coarsen(r, tmp)):
            ref[:rows, 128 * j : 128 * j + 128] = tile
        rhs = ref[...]
    y = smooth(ops[2], rhs, None, chebyshev_terms(coarse_count, COARSE_LOW, COARSE_HIGH))
    for level, width in ((3, w3), (2, w2)):
        op = ops[level - 2]
        rhs, x = kept[level - 2]
        rows = n_sub if level == 3 else 2 * n_sub
        y = x + op[6] * prolong(y, 0, rows, tmp_up, width)
        y = smooth(op, rhs, y, terms)

    for k in range(n_sub):
        y2[k + 1] = y[4 * k : 4 * k + 4]
    y = jnp.concatenate([y2[s][2:4], y2[s + 1], y2[s + 2][0:2]], axis=0)

    def put_x1(d):
        x1[slice(12, 15) if d == 0 else slice(1, 4), :] = x1_r[d]

    row_wait(2, put_x1)
    y = x1[...] + op1[6] * prolong(y, 0, 8, tmp_up, w1)
    y = smooth(op1, fl1, y, terms)

    def put_x0(d):
        x0[slice(20, 22) if d == 0 else slice(2, 4), :] = x0_r[d]

    row_wait(0, put_x0)
    y = x0[...] + op0[6] * prolong(y, 2, 12, tmp_up, w0)
    y = smooth(op0, f0[...], y, terms)
    out[...] = y[4:20, halo : halo + own]

    for d in range(8):
        @pl.when(exists(*DIRS[d]))
        def _():
            a_copy(d).wait_send()
    for d in (0, 1, 4, 5, 6, 7):
        @pl.when(exists(*DIRS[d]))
        def _():
            b_copy(d).wait_send()
    for e in range(3):
        for d in range(2):
            @pl.when(exists(*DIRS[d]))
            def _():
                row_copy(e, d).wait_send()
    for e in range(2):
        for other in range(n_sub):
            @pl.when(s != other)
            def _():
                gather_copy(e, other, s).wait_send()


def body(conductance, source_mask, ground_mask, nodata_mask):
    n_sub, n_blk = lax.axis_size("sub"), lax.axis_size("blk")
    rows, own = conductance.shape
    assert rows == 16 and own % 256 == 0
    coarse_count = 8 + n_sub // 2
    need = coarse_count + 2
    for _ in range(LEVELS - 1):
        need = 2 * need + 2
    halo = round_up(need, 256)
    assert halo <= own
    w0 = own + 2 * halo
    widths = (w0,) + tuple(round_up(w0 >> l, 128) for l in range(1, 5))
    w1, w2, w3, w4 = widths[1:]
    f32 = lambda *shape: pltpu.VMEM(shape, jnp.float32)
    i32 = lambda *shape: pltpu.VMEM(shape, jnp.int32)
    sem = lambda *shape: pltpu.SemaphoreType.DMA(shape)
    r2, r3, r4 = 4 * n_sub, max(2 * n_sub, 8), max(n_sub, 8)
    tmp_rows = max(32 * w0 // 128, 4 * n_sub * round_up(w2, 256) // 128)
    up_rows = max(24 * w0 // 128, 4 * n_sub * w2 // 128)
    vmem = pl.BlockSpec(memory_space=pltpu.VMEM)
    args = (conductance, source_mask, ground_mask, nodata_mask)
    args = [pltpu.with_memory_space_constraint(v, pltpu.HBM) for v in args]
    return pl.pallas_call(
        functools.partial(kernel, (n_sub, n_blk, halo, widths, coarse_count)),
        out_shape=jax.ShapeDtypeStruct((rows, own), jnp.float32),
        in_specs=[pl.BlockSpec(memory_space=pltpu.HBM)] * 4,
        out_specs=vmem,
        scratch_shapes=[
            f32(rows, own), i32(rows, own), i32(rows, own), i32(rows, own), sem(4),
            f32(24, w0), f32(24, w0), f32(24, w0), f32(24, w0),
            f32(16, w1), f32(16, w1), f32(16, w1), f32(16, w1),
            f32(r2, w2), f32(r2, w2), f32(r2, w2), f32(n_sub + 2, 4, w2),
            f32(r3, w3), f32(r4, w4), f32(tmp_rows, 128), f32(up_rows, 128),
            f32(2, 8, own), f32(2, 8, own), f32(2, 48, halo), f32(2, 48, halo),
            f32(4, 8, halo), f32(4, 8, halo), sem(2, 8),
            f32(2, 8, own // 2), f32(2, 8, own // 2), f32(4, 8, halo // 2), f32(4, 8, halo // 2), sem(2, 8),
            f32(2, 2, w0), f32(2, 2, w0),
            f32(2, 2, w1), f32(2, 2, w1), f32(2, 3, w1), f32(2, 3, w1), sem(2, 3, 2),
            f32(n_sub, 8, w2), f32(n_sub, 4, w2), sem(2, 2, n_sub),
        ],
        compiler_params=pltpu.CompilerParams(
            collective_id=0, has_side_effects=True, vmem_limit_bytes=40 * 1024 * 1024
        ),
    )(*args)


def solution(mesh):
    spec = P(("groups", "sub"), "blk")
    return jax.shard_map(
        body, mesh=mesh, in_specs=(spec,) * 4, out_specs=spec, check_vma=False
    )
```

profile of v0, /device:TPU:0, one launch (start us, length us, event | category | flops | bytes accessed | tf_op | source)
XLA Modules:
  0.0 20.3 jit_solution(511792052163068695)
XLA Ops:
  0.0 19.7 %shard_map.46 = f32[16,2048]{1,0:T(8,128)S(1)} custom-call(f32[16,2048]{1,0:T(8,128)} %cond_h.1, s32[16,2048]{1,0:T(8,128)} %src_h.1, s32[16,2048]{1,0:T(8,128)} %gnd_h.1, s32[16,2048]{1,0:T(8,128)} %nod_h.1), custom_call_target="tpu_custom_call" | custom-call | tf_op jit(solution)/shard_map/pallas_call | solution.py:447
  19.7 0.7 %copy.6 = f32[16,2048]{1,0:T(8,128)} copy(f32[16,2048]{1,0:T(8,128)S(1)} %shard_map.46) | data formatting | bytes 262144
where the time goes:
time: 20.5 us; the launch traced here: 20.3 us
  Pallas kernels  19.7 us (96%)
  local copies, waits for them, and re-layouts  0.66 us (3%)
    pallas_call x1, Pallas kernels, body(): pl.pallas_call(functools.partial(kernel, (n_sub, n_blk, halo, widths, coa...  19.7 us
    unnamed x1, local copies, waits for them, and re-layouts  0.66 us

commit v1 on v0

--- a/solution.py
+++ b/solution.py
@@ -55,9 +55,9 @@
 
 def residual(op, f, x):
     e_r, e_l, e_d, e_u, diag, inv, m = op
-    out = f - diag * x
-    out = out + e_r * rolled(x, -1, 1) + e_l * rolled(x, 1, 1)
-    return out + e_d * rolled(x, -1, 0) + e_u * rolled(x, 1, 0)
+    across = e_r * rolled(x, -1, 1) + e_l * rolled(x, 1, 1)
+    along = e_d * rolled(x, -1, 0) + e_u * rolled(x, 1, 0)
+    return (f - diag * x) + (across + along)
 
 
 def smooth(op, f, x, terms):
@@ -100,17 +100,17 @@
     return [s[half * j : half * (j + 1)] for j in range(k)]
 
 
-def prolong(x, first, rows, tmp, cols):
-    n = cols // 128
+def prolong(x, first, rows, tmp, cols, skip=0):
+    n = cols // 128 + skip
     for j in range(x.shape[1] // 128):
         tile = x[:, 128 * j : 128 * j + 128]
         for side in range(2):
-            if 2 * j + side < n:
+            if skip <= 2 * j + side < n:
                 base = 2 * rows * (2 * j + side)
                 v = lane_take(tile, 1 + side)[first : first + rows]
                 tmp[pl.ds(base, rows, stride=2), :] = v
                 tmp[pl.ds(base + 1, rows, stride=2), :] = v
-    return jnp.concatenate([tmp[2 * rows * j : 2 * rows * (j + 1), :] for j in range(n)], axis=1)
+    return jnp.concatenate([tmp[2 * rows * j : 2 * rows * (j + 1), :] for j in range(skip, n)], axis=1)
 
 
 def kernel(
@@ -164,23 +164,17 @@
     c = cond[...] * valid
     g = gnd[...].astype(jnp.float32) * c
     f = valid * (src[...].astype(jnp.float32) - 0.125)
-    c0[4:20, halo : halo + own] = c
-    g0[4:20, halo : halo + own] = g
-    f0[4:20, halo : halo + own] = f
-    for i, (rc, rg) in enumerate(((slice(0, 3), slice(0, 2)), (slice(13, 16), slice(14, 16)))):
-        a_row_s[i, 0:3] = c[rc]
-        a_row_s[i, 3:5] = g[rg]
-        a_row_s[i, 5:7] = f[rg]
-        a_row_s[i, 7:8] = jnp.zeros((1, own), jnp.float32)
-        for j, lanes in enumerate((slice(0, halo), slice(own - halo, own))):
-            a_cor_s[2 * i + j, 0:3] = c[rc, lanes]
-            a_cor_s[2 * i + j, 3:5] = g[rg, lanes]
-            a_cor_s[2 * i + j, 5:7] = f[rg, lanes]
-            a_cor_s[2 * i + j, 7:8] = jnp.zeros((1, halo), jnp.float32)
-    for j, lanes in enumerate((slice(0, halo), slice(own - halo, own))):
-        a_col_s[j, 0:16] = c[:, lanes]
-        a_col_s[j, 16:32] = g[:, lanes]
-        a_col_s[j, 32:48] = f[:, lanes]
+    edges = ((slice(0, 3), slice(0, 2)), (slice(13, 16), slice(14, 16)))
+    sides = (slice(0, halo), slice(own - halo, own))
+
+    def stage(ref, rc, rg, lanes):
+        ref[0:3] = c[rc, lanes]
+        ref[3:5] = g[rg, lanes]
+        ref[5:7] = f[rg, lanes]
+        ref[7:8] = jnp.zeros((1, ref.shape[1]), jnp.float32)
+
+    for i in range(2):
+        stage(a_row_s.at[i], *edges[i], slice(0, own))
 
     has = lambda flag: jnp.where(flag, 1, 0)
     partners = n_sub - 1
@@ -242,16 +236,42 @@
             def _():
                 gather_copy(e, other, s).start()
 
+    def row_done(e):
+        for d in range(2):
+            @pl.when(exists(*DIRS[d]))
+            def _():
+                row_copy(e, d).wait_send()
+
+    def gather_done(e):
+        for other in range(n_sub):
+            @pl.when(s != other)
+            def _():
+                gather_copy(e, other, s).wait_send()
+
     def gather_wait(e):
         for other in range(n_sub):
             @pl.when(s != other)
             def _():
                 gather_copy(e, other, other).wait_recv()
 
-    for d in range(8):
-        @pl.when(exists(*DIRS[d]))
-        def _():
-            a_copy(d).start()
+    def a_start(which):
+        for d in which:
+            @pl.when(exists(*DIRS[d]))
+            def _():
+                a_copy(d).start()
+
+    a_start((0, 1))
+    for j, lanes in enumerate(sides):
+        for k, v in enumerate((c, g, f)):
+            a_col_s[j, 16 * k : 16 * k + 16] = v[:, lanes]
+    a_start((2, 3))
+    for i in range(2):
+        for j, lanes in enumerate(sides):
+            stage(a_cor_s.at[2 * i + j], *edges[i], lanes)
+    a_start((4, 5, 6, 7))
+    c0[4:20, halo : halo + own] = c
+    g0[4:20, halo : halo + own] = g
+    f0[4:20, halo : halo + own] = f
 
     h1, own1 = halo // 2, own // 2
     both = jnp.concatenate([0.25 * c, g], axis=0)
@@ -337,6 +357,16 @@
     x1_s[0] = x[4:7]
     x1_s[1] = x[9:12]
     row_start(2)
+
+    for d in range(8):
+        @pl.when(exists(*DIRS[d]))
+        def _():
+            a_copy(d).wait_send()
+            if d not in (2, 3):
+                b_copy(d).wait_send()
+    row_done(0)
+    row_done(1)
+    gather_done(0)
 
     gather_wait(0)
     for k in range(n_sub):
@@ -398,28 +428,14 @@
         x0[slice(20, 22) if d == 0 else slice(2, 4), :] = x0_r[d]
 
     row_wait(0, put_x0)
-    y = x0[...] + op0[6] * prolong(y, 2, 12, tmp_up, w0)
-    y = smooth(op0, f0[...], y, terms)
-    out[...] = y[4:20, halo : halo + own]
-
-    for d in range(8):
-        @pl.when(exists(*DIRS[d]))
-        def _():
-            a_copy(d).wait_send()
-    for d in (0, 1, 4, 5, 6, 7):
-        @pl.when(exists(*DIRS[d]))
-        def _():
-            b_copy(d).wait_send()
-    for e in range(3):
-        for d in range(2):
-            @pl.when(exists(*DIRS[d]))
-            def _():
-                row_copy(e, d).wait_send()
-    for e in range(2):
-        for other in range(n_sub):
-            @pl.when(s != other)
-            def _():
-                gather_copy(e, other, s).wait_send()
+    near = slice(halo - 128, halo + own + 128)
+    op0 = [v[:, near] for v in op0]
+    y = prolong(y, 2, 12, tmp_up, own + 256, halo // 128 - 1)
+    y = smooth(op0, f0[:, near], x0[:, near] + op0[6] * y, terms)
+    out[...] = y[4:20, 128 : 128 + own]
+
+    row_done(2)
+    gather_done(1)
 
 
 def body(conductance, source_mask, ground_mask, nodata_mask):

time: 20.5 us -> 20.4 us (level)
  no operation moved by 1% of the time
where the time goes in v1:
time: 20.4 us; the launch traced here: 20.3 us
  Pallas kernels  19.6 us (96%)
  local copies, waits for them, and re-layouts  0.66 us (3%)
    pallas_call x1, Pallas kernels, body(): pl.pallas_call(functools.partial(kernel, (n_sub, n_blk, halo, widths, coa...  19.6 us
    unnamed x1, local copies, waits for them, and re-layouts  0.66 us

profile of v1, /device:TPU:0, one launch (start us, length us, event | category | flops | bytes accessed | tf_op | source)
XLA Modules:
  0.0 20.3 jit_solution(10993934833410138001)
XLA Ops:
  0.0 19.6 %shard_map.46 = f32[16,2048]{1,0:T(8,128)S(1)} custom-call(f32[16,2048]{1,0:T(8,128)} %cond_h.1, s32[16,2048]{1,0:T(8,128)} %src_h.1, s32[16,2048]{1,0:T(8,128)} %gnd_h.1, s32[16,2048]{1,0:T(8,128)} %nod_h.1), custom_call_target="tpu_custom_call" | custom-call | tf_op jit(solution)/shard_map/pallas_call | solution.py:463
  19.6 0.7 %copy.6 = f32[16,2048]{1,0:T(8,128)} copy(f32[16,2048]{1,0:T(8,128)S(1)} %shard_map.46) | data formatting | bytes 262144

commit v2 on v1

--- a/solution.py
+++ b/solution.py
@@ -34,36 +34,49 @@
     return pltpu.roll(x, shift % x.shape[axis], axis)
 
 
-def level_operator(c, g, whole_rows):
+def row_neighbours(x, spare):
+    if spare is None:
+        return rolled(x, 1, 0), rolled(x, -1, 0)
+    rows, tiles = x.shape[0], x.shape[1] // 128
+    for t in range(tiles):
+        spare[t, 8 : 8 + rows, :] = x[:, 128 * t : 128 * t + 128]
+    return [
+        jnp.concatenate([spare[t, at : at + rows, :] for t in range(tiles)], axis=1)
+        for at in (7, 9)
+    ]
+
+
+def level_operator(c, g, whole_rows, spare=None):
     rows, cols = c.shape
     h = 0.5 * c
     valid = c > 0.0
     c_r = rolled(c, -1, 1)
-    c_d = rolled(c, -1, 0)
+    c_d = row_neighbours(c, spare)[1]
     e_r = jnp.where(valid & (c_r > 0.0), h + 0.5 * c_r, 0.0)
     ok_d = valid & (c_d > 0.0)
     if whole_rows:
         ok_d = ok_d & (lax.broadcasted_iota(jnp.int32, c.shape, 0) < rows - 1)
     e_d = jnp.where(ok_d, h + 0.5 * c_d, 0.0)
     e_l = rolled(e_r, 1, 1)
-    e_u = rolled(e_d, 1, 0)
+    e_u = row_neighbours(e_d, spare)[0]
     m = jnp.where(valid, 1.0, 0.0)
     diag = e_d + e_u + e_r + e_l + g + (1.0 - m)
     inv = 1.0 / jnp.maximum(diag, 0.25 * c)
     return e_r, e_l, e_d, e_u, diag, inv, m
 
 
-def residual(op, f, x):
+def residual(op, f, x, spare=None):
     e_r, e_l, e_d, e_u, diag, inv, m = op
     across = e_r * rolled(x, -1, 1) + e_l * rolled(x, 1, 1)
-    along = e_d * rolled(x, -1, 0) + e_u * rolled(x, 1, 0)
+    x_u, x_d = row_neighbours(x, spare)
+    along = e_d * x_d + e_u * x_u
     return (f - diag * x) + (across + along)
 
 
-def smooth(op, f, x, terms):
+def smooth(op, f, x, terms, spare=None):
     d = None
     for keep, fresh in terms:
-        r = f if x is None else residual(op, f, x)
+        r = f if x is None else residual(op, f, x, spare)
         step = fresh * (r * op[5])
         d = step if d is None else keep * d + step
         x = d if x is None else x + d
@@ -116,7 +129,7 @@
 def kernel(
     plan,
     cond_h, src_h, gnd_h, nod_h, out, cond, nod, gnd, src, in_sem,
-    c0, g0, f0, x0, c1, g1, f1, x1, c2, g2, f2, y2, f3, f4, tmp, tmp_up,
+    spare0, spare1, c0, g0, f0, x0, c1, g1, f1, x1, c2, g2, f2, y2, f3, f4, tmp, tmp_up,
     a_row_s, a_row_r, a_col_s, a_col_r, a_cor_s, a_cor_r, a_sem,
     b_row_s, b_row_r, b_cor_s, b_cor_r, b_sem,
     x0_s, x0_r, f1_s, f1_r, x1_s, x1_r, row_sem,
@@ -155,7 +168,7 @@
                 barrier, 1, device_id={"sub": s + dr, "blk": b + dc}, device_id_type=MESH
             )
 
-    for ref in (c0, g0, f0, c1, g1, f1, y2, f3, f4):
+    for ref in (spare0, spare1, c0, g0, f0, c1, g1, f1, y2, f3, f4):
         ref[...] = jnp.zeros_like(ref)
 
     for load in loads:
@@ -308,10 +321,10 @@
                 f0[near, lanes] = got[5:7]
 
     terms = chebyshev_terms(*SMOOTH)
-    op0 = level_operator(c0[...], g0[...], False)
+    op0 = level_operator(c0[...], g0[...], False, spare0)
     f = f0[...]
-    x = smooth(op0, f, None, terms)
-    r = residual(op0, f, x)
+    x = smooth(op0, f, None, terms, spare0)
+    r = residual(op0, f, x, spare0)
     rhs = jnp.concatenate(coarsen(r[4:20], tmp), axis=1)
     f1[4:12, :] = rhs
     f1_s[0] = rhs[0:2]
@@ -342,15 +355,15 @@
             got = b_row_r.at[d] if d < 2 else b_cor_r.at[d - 4]
             c1[slice(1, 4) if dr > 0 else slice(12, 15), lanes] = got[0:3]
             g1[slice(2, 4) if dr > 0 else slice(12, 14), lanes] = got[3:5]
-    op1 = level_operator(c1[...], g1[...], False)
+    op1 = level_operator(c1[...], g1[...], False, spare1)
 
     def put_f1(d):
         f1[slice(12, 14) if d == 0 else slice(2, 4), :] = f1_r[d]
 
     row_wait(1, put_f1)
     fl1 = f1[...]
-    x = smooth(op1, fl1, None, terms)
-    r = residual(op1, fl1, x)
+    x = smooth(op1, fl1, None, terms, spare1)
+    r = residual(op1, fl1, x, spare1)
     f2_g[s] = jnp.concatenate(coarsen(r[4:12], tmp), axis=1)
     gather_start(1)
     x1[...] = x
@@ -422,7 +435,7 @@
 
     row_wait(2, put_x1)
     y = x1[...] + op1[6] * prolong(y, 0, 8, tmp_up, w1)
-    y = smooth(op1, fl1, y, terms)
+    y = smooth(op1, fl1, y, terms, spare1)
 
     def put_x0(d):
         x0[slice(20, 22) if d == 0 else slice(2, 4), :] = x0_r[d]
@@ -431,7 +444,7 @@
     near = slice(halo - 128, halo + own + 128)
     op0 = [v[:, near] for v in op0]
     y = prolong(y, 2, 12, tmp_up, own + 256, halo // 128 - 1)
-    y = smooth(op0, f0[:, near], x0[:, near] + op0[6] * y, terms)
+    y = smooth(op0, f0[:, near], x0[:, near] + op0[6] * y, terms, spare0)
     out[...] = y[4:20, 128 : 128 + own]
 
     row_done(2)
@@ -467,6 +480,7 @@
         out_specs=vmem,
         scratch_shapes=[
             f32(rows, own), i32(rows, own), i32(rows, own), i32(rows, own), sem(4),
+            f32(w0 // 128, 40, 128), f32(w1 // 128, 32, 128),
             f32(24, w0), f32(24, w0), f32(24, w0), f32(24, w0),
             f32(16, w1), f32(16, w1), f32(16, w1), f32(16, w1),
             f32(r2, w2), f32(r2, w2), f32(r2, w2), f32(n_sub + 2, 4, w2),

time: 20.4 us -> 20.4 us (level)
  no operation moved by 1% of the time
where the time goes in v2:
time: 20.4 us; the launch traced here: 20.3 us
  Pallas kernels  19.6 us (96%)
  local copies, waits for them, and re-layouts  0.66 us (3%)
    pallas_call x1, Pallas kernels, body(): pl.pallas_call(functools.partial(kernel, (n_sub, n_blk, halo, widths, coa...  19.6 us
    unnamed x1, local copies, waits for them, and re-layouts  0.66 us

profile of v2, /device:TPU:0, one launch (start us, length us, event | category | flops | bytes accessed | tf_op | source)
XLA Modules:
  0.0 20.3 jit_solution(546928211115746815)
XLA Ops:
  0.0 19.6 %shard_map.46 = f32[16,2048]{1,0:T(8,128)S(1)} custom-call(f32[16,2048]{1,0:T(8,128)} %cond_h.1, s32[16,2048]{1,0:T(8,128)} %src_h.1, s32[16,2048]{1,0:T(8,128)} %gnd_h.1, s32[16,2048]{1,0:T(8,128)} %nod_h.1), custom_call_target="tpu_custom_call" | custom-call | tf_op jit(solution)/shard_map/pallas_call | solution.py:476
  19.6 0.7 %copy.6 = f32[16,2048]{1,0:T(8,128)} copy(f32[16,2048]{1,0:T(8,128)S(1)} %shard_map.46) | data formatting | bytes 262144

commit v3 on v1

--- a/solution.py
+++ b/solution.py
@@ -231,7 +231,7 @@
         )
 
     def gather_start(e):
-        for other in range(n_sub):
+        for other in sorted(range(n_sub), key=lambda k: -abs(2 * k - n_sub + 1)):
             @pl.when(s != other)
             def _():
                 gather_copy(e, other, s).start()
@@ -388,6 +388,15 @@
             parts.append(v)
         cg = tuple(parts)
         ops.append(level_operator(*cg, True))
+
+    def put_x0(d):
+        x0[slice(20, 22) if d == 0 else slice(2, 4), :] = x0_r[d]
+
+    row_wait(0, put_x0)
+    def put_x1(d):
+        x1[slice(12, 15) if d == 0 else slice(1, 4), :] = x1_r[d]
+
+    row_wait(2, put_x1)
 
     gather_wait(1)
     for k in range(n_sub):
@@ -417,17 +426,9 @@
         y2[k + 1] = y[4 * k : 4 * k + 4]
     y = jnp.concatenate([y2[s][2:4], y2[s + 1], y2[s + 2][0:2]], axis=0)
 
-    def put_x1(d):
-        x1[slice(12, 15) if d == 0 else slice(1, 4), :] = x1_r[d]
-
-    row_wait(2, put_x1)
     y = x1[...] + op1[6] * prolong(y, 0, 8, tmp_up, w1)
     y = smooth(op1, fl1, y, terms)
 
-    def put_x0(d):
-        x0[slice(20, 22) if d == 0 else slice(2, 4), :] = x0_r[d]
-
-    row_wait(0, put_x0)
     near = slice(halo - 128, halo + own + 128)
     op0 = [v[:, near] for v in op0]
     y = prolong(y, 2, 12, tmp_up, own + 256, halo // 128 - 1)

time: 20.4 us -> 20.3 us (level)
  no operation moved by 1% of the time
where the time goes in v3:
time: 20.3 us; the launch traced here: 20.2 us
  Pallas kernels  19.5 us (96%)
  local copies, waits for them, and re-layouts  0.66 us (3%)
    pallas_call x1, Pallas kernels, body(): pl.pallas_call(functools.partial(kernel, (n_sub, n_blk, halo, widths, coa...  19.5 us
    unnamed x1, local copies, waits for them, and re-layouts  0.66 us

profile of v3, /device:TPU:0, one launch (start us, length us, event | category | flops | bytes accessed | tf_op | source)
XLA Modules:
  0.0 20.2 jit_solution(3324230210296482785)
XLA Ops:
  0.0 19.5 %shard_map.46 = f32[16,2048]{1,0:T(8,128)S(1)} custom-call(f32[16,2048]{1,0:T(8,128)} %cond_h.1, s32[16,2048]{1,0:T(8,128)} %src_h.1, s32[16,2048]{1,0:T(8,128)} %gnd_h.1, s32[16,2048]{1,0:T(8,128)} %nod_h.1), custom_call_target="tpu_custom_call" | custom-call | tf_op jit(solution)/shard_map/pallas_call | solution.py:464
  19.5 0.7 %copy.6 = f32[16,2048]{1,0:T(8,128)} copy(f32[16,2048]{1,0:T(8,128)S(1)} %shard_map.46) | data formatting | bytes 262144
